TPU v7x, 128 devices: a whole 4x4x4 slice. The times are simulated.
128 devices in a mesh: lev: 4 (over y), col: 32 (over x, z, core).
Axes of the slice: x: 4, y: 4, z: 4, core: 2. Of those that a mesh axis runs over, the one named last changes fastest.
Arguments:
- increment: bfloat16 [3, 128, 131072], P(None, 'lev', 'col'), may hold values from -6 to 6
- jacobian: bfloat16 [1024, 616, 384], P(('lev', 'col')), may hold values from -0.3125 to 0.3125
- departure: bfloat16 [616, 1048576], P(None, ('lev', 'col')), may hold values from -6 to 6
- predictor: float32 [8, 1048576], P(None, ('lev', 'col')), may hold values from -5 to 5
- bias_coef: float32 [616, 8], replicated, may hold values from -1.5 to 1.5
- obs_sigma: float32 [616], replicated, may hold values from 0.5 to 2
- channel_use: int32 [1024, 616], P(('lev', 'col')), may hold values 0 or 1
- send_cols: int32 [128, 128, 8], P(('lev', 'col')), may hold values from 0 to 1023
- obs_slot: int32 [1048576], P(('lev', 'col')), may hold values from 0 to 1023, as said below
Outputs:
- gradient: float32 [3, 128, 131072], P(None, 'lev', 'col')
Inputs may be any that keep to these rules, and one draw needn't show every extreme that they name: obs_slot[j] = s * 8 + k; the slots (s, p, k) named by the observations of device p are, for each s, the first few of the 8, at least 2 of them; some device p names all 8 slots of every device.
All inputs are finite; a program needn't handle non-finite values. No bound on the sum of `channel_use` on one device may be relied on, other than what follows from the above.
Results may differ from a plain program's by a relative error of at most 0.001.
Values may be sent and summed in bfloat16 or wider, within the bound.
A program may use at most 128 MiB of HBM per device.

v0:
```python
import jax
import jax.numpy as jnp
from jax import lax
from jax.sharding import PartitionSpec as P


def fetch_rows(outgoing):
    return lax.all_to_all(outgoing, ("lev", "col"), split_axis=0, concat_axis=0, tiled=True)


def return_rows(outgoing):
    return lax.all_to_all(outgoing, ("lev", "col"), split_axis=0, concat_axis=0, tiled=True)


def observe(profile, jacobian, departure, predictor, bias_coef, obs_sigma, channel_use):
    tile_count = jacobian.shape[0]
    channels = jacobian.shape[1]
    obs_count = profile.shape[0]
    profile_len = profile.shape[1]
    obs_tile = obs_count // tile_count
    tangent = jnp.einsum(
        "tcf,tof->cto",
        jacobian,
        profile.reshape(tile_count, obs_tile, profile_len),
        preferred_element_type=jnp.float32,
    )
    bias_term = jnp.dot(
        bias_coef, predictor, precision=lax.Precision.HIGHEST, preferred_element_type=jnp.float32
    )
    residual = tangent - (departure.astype(jnp.float32) - bias_term).reshape(
        channels, tile_count, obs_tile
    )
    inverse_var = 1.0 / (obs_sigma * obs_sigma)
    scaling = channel_use.astype(jnp.float32).T * inverse_var[:, None]
    forcing = (scaling[:, :, None] * residual).astype(jnp.bfloat16)
    return jnp.einsum(
        "tcf,cto->tof", jacobian, forcing, preferred_element_type=jnp.float32
    ).reshape(obs_count, profile_len)


def on_device(
    increment,
    jacobian,
    departure,
    predictor,
    bias_coef,
    obs_sigma,
    channel_use,
    send_cols,
    obs_slot,
):
    lev_size = lax.axis_size("lev")
    col_size = lax.axis_size("col")
    peer_count = lev_size * col_size
    field_count = increment.shape[0]
    capacity = send_cols.shape[2]
    columns = lax.all_to_all(increment, "lev", split_axis=2, concat_axis=1, tiled=True)
    level_count = columns.shape[1]
    column_count = columns.shape[2]
    profile_len = field_count * level_count
    column_rows = columns.reshape(profile_len, column_count).T
    slot_lists = send_cols[0]
    outgoing = column_rows[slot_lists]
    incoming = fetch_rows(outgoing).reshape(peer_count * capacity, profile_len)
    profile = incoming[obs_slot]
    adjoint = observe(profile, jacobian, departure, predictor, bias_coef, obs_sigma, channel_use)
    slot_adjoint = jax.ops.segment_sum(adjoint, obs_slot, num_segments=peer_count * capacity)
    returned = return_rows(slot_adjoint.reshape(peer_count, capacity, profile_len))
    column_adjoint = jax.ops.segment_sum(
        returned.reshape(peer_count * capacity, profile_len),
        slot_lists.reshape(-1),
        num_segments=column_count,
    )
    field_adjoint = column_adjoint.T.reshape(field_count, level_count, column_count)
    return lax.all_to_all(field_adjoint, "lev", split_axis=1, concat_axis=2, tiled=True)


def solution(mesh):
    return jax.shard_map(
        on_device,
        mesh=mesh,
        in_specs=(
            P(None, "lev", "col"),
            P(("lev", "col"), None, None),
            P(None, ("lev", "col")),
            P(None, ("lev", "col")),
            P(),
            P(),
            P(("lev", "col"), None),
            P(("lev", "col"), None, None),
            P(("lev", "col")),
        ),
        out_specs=P(None, "lev", "col"),
        check_vma=False,
    )
```

profile of v0, /device:TPU:0, one launch (start us, length us, event | category | flops | bytes accessed | tf_op | source)
XLA Modules:
  0.0 255.4 jit_solution(5134098283058532032)
XLA Ops:
  0.0 0.0 copy-start
  0.0 6.0 %copy.31 = bf16[3,32,4096]{1,0,2:T(4,128)(2,1)} copy(bf16[3,32,4096]{2,1,0:T(8,128)(2,1)} %param.9) | data formatting | bytes 1572864 | tf_op args[0]
  6.0 0.0 copy-start.5
  6.0 0.0 copy-start.6
  6.0 0.0 copy-start.4
  6.0 0.0 copy-start.2
  6.0 5.6 %reshape.103 = bf16[4,2,49152]{2,1,0:T(2,128)(2,1)} reshape(bf16[4096,3,32]{2,1,0:T(4,128)(2,1)} %bitcast.49) | data formatting | bytes 1572864
  11.6 4.5 %all-to-all-start = ((bf16[4,2,49152]{2,1,0:T(2,128)(2,1)}), bf16[4,2,49152]{2,1,0:T(2,128)(2,1)S(1)}, u32[]{:S(2)}, u32[]{:S(2)}) async-start(bf16[4,2,49152]{2,1,0:T(2,128)(2,1)} %reshape.103), calls=%async_computation | async-start | bytes 1572864 | tf_op jit(solution)/shard_map/all_to_all | solution.py:57
  16.2 0.0 copy-done.5
  16.2 0.1 copy.35
  16.3 0.1 reshape.65
  16.4 0.0 copy-done.6
  16.4 0.0 copy-done.4
  16.4 0.0 copy-done.2
  16.5 12.0 %all-to-all-done = bf16[4,2,49152]{2,1,0:T(2,128)(2,1)S(1)} async-done(((bf16[4,2,49152]{2,1,0:T(2,128)(2,1)}), bf16[4,2,49152]{2,1,0:T(2,128)(2,1)S(1)}, u32[]{:S(2)}, u32[]{:S(2)}) %all-to-all-start) | async-done | bytes 786464 | tf_op jit(solution)/shard_map/all_to_all | solution.py:57
  28.5 4.2 %reshape.104 = bf16[4096,3,32]{2,1,0:T(4,128)(2,1)} reshape(bf16[4,2,49152]{2,1,0:T(2,128)(2,1)S(1)} %all-to-all-done) | data formatting | bytes 1572864
  32.6 5.3 %copy.33 = bf16[3,4,32,1024]{3,2,1,0:T(8,128)(2,1)S(1)} copy(bf16[3,4,32,1024]{2,0,3,1:T(4,128)(2,1)} %bitcast.48) | data formatting | bytes 1572864 | tf_op jit(solution)/shard_map/all_to_all | solution.py:57
  38.0 0.4 copy.34
  38.3 0.0 copy-start.3
  38.4 5.0 %gather_fusion = bf16[1024,384]{1,0:T(8,128)(2,1)} fusion(bf16[1024,384]{1,0:T(8,128)(2,1)S(1)} %bitcast.46, s32[1024]{0:T(1024)S(1)} %broadcast_clamp_fusion), kind=kCustom, calls=%fused_computation | custom fusion | bytes 1576960 | tf_op jit(solution)/shard_map/gather | solution.py:63
  43.4 9.2 %all-to-all-start.1 = ((bf16[128,8,384]{2,1,0:T(8,128)(2,1)}), bf16[128,8,384]{2,1,0:T(8,128)(2,1)S(1)}, u32[]{:S(2)}, u32[]{:S(2)}) async-start(bf16[128,8,384]{2,1,0:T(8,128)(2,1)} %bitcast.7), calls=%async_computation.1 | async-start | bytes 1572864 | tf_op jit(solution)/shard_map/all_to_all | solution.py:8
  52.6 0.0 copy-done
  52.6 0.0 copy-done.3
  52.6 20.8 %convert_subtract_fusion = f32[616,8192]{1,0:T(8,128)} fusion(bf16[616,8192]{1,0:T(8,128)(2,1)} %param.11, f32[616,8]{0,1:T(8,128)S(1)} %copy-done.3, f32[8,8192]{1,0:T(8,128)S(1)} %copy-done), kind=kOutput, calls=%fused_computation.7 | convolution fusion | flops 494534656 | bytes 30559488 | tf_op jit(solution)/shard_map/dot_general | solution.py:27
  73.4 0.0 all-to-all-done.1
  73.4 33.1 %gather_fusion.1 = bf16[8192,384]{1,0:T(8,128)(2,1)} fusion(bf16[1024,384]{1,0:T(8,128)(2,1)S(1)} %bitcast.45, s32[8192]{0:T(1024)S(1)} %fusion.12), kind=kCustom, calls=%fused_computation.1 | custom fusion | bytes 12615680 | tf_op jit(solution)/shard_map/gather | solution.py:65
  106.5 24.5 %fusion.2 = f32[8,1024,384]{2,1,0:T(8,128)} fusion(bf16[8,616,384]{2,1,0:T(8,128)(2,1)} %param.10, f32[77,8,8,1024]{3,2,1,0:T(8,128)} %bitcast.47, f32[616,8]{0,1:T(8,128)S(1)} %multiply_bitcast_fusion, bf16[8,1024,384]{2,1,0:T(8,128)(2,1)} %bitcast.50), kind=kOutput, calls=%fused_computation.8 | convolution fusion | flops 7766212608 | bytes 42863872 | tf_op jit(solution)/shard_map/tcf,cto->tof/dot_general | solution.py:36
  131.0 50.4 %scatter_custom_fusion = f32[1024,384]{1,0:T(8,128)} fusion(s32[8192]{0:T(1024)S(1)} %copy-done.2, f32[8192,384]{1,0:T(8,128)} %bitcast.55, f32[]{:T(128)} %constant.4.clone.1), kind=kCustom, calls=%fused_computation.14 | custom fusion | flops 3145728 | bytes 1573376 | tf_op jit(solution)/shard_map/scatter-add | solution.py:67
  181.5 9.6 %all-to-all-start.2 = ((f32[128,8,384]{2,1,0:T(8,128)}), f32[128,8,384]{2,1,0:T(8,128)S(1)}, u32[]{:S(2)}, u32[]{:S(2)}) async-start(f32[128,8,384]{2,1,0:T(8,128)} %bitcast.12), calls=%async_computation.2 | async-start | bytes 3145728 | tf_op jit(solution)/shard_map/all_to_all | solution.py:12
  191.0 0.1 copy.30
  191.1 0.1 reshape.89
  191.2 24.7 %all-to-all-done.2 = f32[128,8,384]{2,1,0:T(8,128)S(1)} async-done(((f32[128,8,384]{2,1,0:T(8,128)}), f32[128,8,384]{2,1,0:T(8,128)S(1)}, u32[]{:S(2)}, u32[]{:S(2)}) %all-to-all-start.2) | async-done | bytes 1572896 | tf_op jit(solution)/shard_map/all_to_all | solution.py:12
  215.9 7.1 %scatter_custom_fusion.1 = f32[1024,384]{1,0:T(8,128)S(1)} fusion(s32[1024]{0:T(1024)S(1)} %reshape.89, f32[128,8,384]{2,1,0:T(8,128)S(1)} %all-to-all-done.2, f32[]{:T(128)} %constant.4.clone.1), kind=kCustom, calls=%fused_computation.11 | custom fusion | flops 393216 | bytes 3145732 | tf_op jit(solution)/shard_map/scatter-add | solution.py:69
  223.0 0.5 copy.37
  223.5 1.1 copy.38
  224.5 0.0 copy-start.1
  224.6 28.6 %all_to_all.43 = f32[3,128,1024]{2,0,1:T(4,128)S(1)} all-to-all(f32[3,128,1024]{2,0,1:T(4,128)S(1)} %copy.38), channel_id=1, replica_groups=mesh['lev'=4,'col'=32] {'lev'}, dimensions={1} | all-to-all | bytes 3145728 | tf_op jit(solution)/shard_map/all_to_all | solution.py:75
  253.2 0.9 copy.39
  254.1 1.3 copy.44
  255.4 0.0 copy-done.1
  (5 shorter events, 0.0 us)
Async XLA Ops:
  0.0 52.6 %copy-start = (f32[8,8192]{1,0:T(8,128)S(1)}, f32[8,8192]{1,0:T(8,128)}, u32[]{:S(2)}) copy-start(f32[8,8192]{1,0:T(8,128)} %param.12) | copy-start | bytes 786436
  6.0 10.1 %copy-start.5 = (s32[1,128,8]{1,2,0:T(8,128)S(1)}, s32[1,128,8]{1,2,0:T(8,128)}, u32[]{:S(2)}) copy-start(s32[1,128,8]{1,2,0:T(8,128)} %param.16) | copy-start | bytes 12292
  6.0 10.4 %copy-start.6 = (f32[616]{0:T(1024)S(1)}, f32[616]{0:T(1024)}, u32[]{:S(2)}) copy-start(f32[616]{0:T(1024)} %param.14) | copy-start | bytes 7396
  6.0 10.4 %copy-start.4 = (s32[8,616]{1,0:T(8,128)S(1)}, s32[8,616]{1,0:T(8,128)}, u32[]{:S(2)}) copy-start(s32[8,616]{1,0:T(8,128)} %param.15) | copy-start | bytes 59140
  6.0 10.4 %copy-start.2 = (s32[8192]{0:T(1024)S(1)}, s32[8192]{0:T(1024)}, u32[]{:S(2)}) copy-start(s32[8192]{0:T(1024)} %param.17) | copy-start | bytes 98308
  11.6 16.8 %all-to-all-start = ((bf16[4,2,49152]{2,1,0:T(2,128)(2,1)}), bf16[4,2,49152]{2,1,0:T(2,128)(2,1)S(1)}, u32[]{:S(2)}, u32[]{:S(2)}) async-start(bf16[4,2,49152]{2,1,0:T(2,128)(2,1)} %reshape.103), calls=%async_computation | async-start | bytes 1572864 | tf_op jit(solution)/shard_map/all_to_all | solution.py:57
  38.3 14.2 %copy-start.3 = (f32[616,8]{0,1:T(8,128)S(1)}, f32[616,8]{0,1:T(8,128)}, u32[]{:S(2)}) copy-start(f32[616,8]{0,1:T(8,128)} %param.13) | copy-start | bytes 59140
  43.4 30.0 %all-to-all-start.1 = ((bf16[128,8,384]{2,1,0:T(8,128)(2,1)}), bf16[128,8,384]{2,1,0:T(8,128)(2,1)S(1)}, u32[]{:S(2)}, u32[]{:S(2)}) async-start(bf16[128,8,384]{2,1,0:T(8,128)(2,1)} %bitcast.7), calls=%async_computation.1 | async-start | bytes 1572864 | tf_op jit(solution)/shard_map/all_to_all | solution.py:8
  181.5 34.5 %all-to-all-start.2 = ((f32[128,8,384]{2,1,0:T(8,128)}), f32[128,8,384]{2,1,0:T(8,128)S(1)}, u32[]{:S(2)}, u32[]{:S(2)}) async-start(f32[128,8,384]{2,1,0:T(8,128)} %bitcast.12), calls=%async_computation.2 | async-start | bytes 3145728 | tf_op jit(solution)/shard_map/all_to_all | solution.py:12
  224.5 30.9 %copy-start.1 = (f32[8,8192]{1,0:T(8,128)S(1)}, f32[8,8192]{1,0:T(8,128)}, u32[]{:S(2)}) copy-start(f32[8,8192]{1,0:T(8,128)} %param.12) | copy-start | bytes 786436
where the time goes:
time: 256 us; the launch traced here: 255 us
  local copies, waits for them, and re-layouts  63.8 us (25%)
  other arithmetic  57.5 us (22%)
  matrix products  45.3 us (18%)
  waiting for transfers between devices  36.7 us (14%)
  blocking collectives  28.6 us (11%)
  starting transfers between devices  23.3 us (9%)
    scatter-add x1, other arithmetic, on_device(): jax.ops.segment_sum(adjoint, obs_slot, num_segments=peer_count * capacity)  50.4 us
    gather x1, local copies, waits for them, and re-layouts, on_device(): profile = incoming[obs_slot]  33.1 us
    all_to_all x1, blocking collectives, on_device(): lax.all_to_all(field_adjoint, 'lev', split_axis=1, concat_axis=2, tiled=T...  28.6 us
    all_to_all x1, waiting for transfers between devices, return_rows(): lax.all_to_all(outgoing, ('lev', 'col'), split_axis=0, concat_axis=0, til...  24.7 us
    dot_general x1, matrix products, observe(): jnp.einsum('tcf,cto->tof', jacobian, forcing, preferred_element_type=jnp....  24.5 us
    dot_general x1, matrix products, observe(): jnp.dot(bias_coef, predictor, precision=lax.Precision.HIGHEST, preferred_...  20.8 us
    unnamed x18, local copies, waits for them, and re-layouts  15.9 us
    all_to_all x1, waiting for transfers between devices, on_device(): lax.all_to_all(increment, 'lev', split_axis=2, concat_axis=1, tiled=True)  12 us
  transfers between devices with their start and end apart: 3, of which 2 were waited for; matrix products, arithmetic and copies ran while one was open for 8% of the time, Pallas kernels for 0%

commit v1 on v0

--- a/solution.py
+++ b/solution.py
@@ -2,6 +2,18 @@
 import jax.numpy as jnp
 from jax import lax
 from jax.sharding import PartitionSpec as P
+
+
+def split_up(shard, dim, devices):
+    dims = shard.shape
+    blocks = shard.reshape(*dims[:dim], devices, dims[dim] // devices, *dims[dim + 1 :])
+    return jnp.moveaxis(blocks, dim, 0)
+
+
+def laid_out(tiles, dim):
+    shape = list(tiles.shape[1:])
+    shape[dim] *= tiles.shape[0]
+    return jnp.moveaxis(tiles, 0, dim).reshape(shape)
 
 
 def fetch_rows(outgoing):
@@ -54,7 +66,14 @@
     peer_count = lev_size * col_size
     field_count = increment.shape[0]
     capacity = send_cols.shape[2]
-    columns = lax.all_to_all(increment, "lev", split_axis=2, concat_axis=1, tiled=True)
+    peers, place = (lax.axis_size("lev"), lax.axis_index("lev"))
+    blocks = split_up(increment, 2, peers)
+    outs = [blocks[place]]
+    for hop in range(1, peers):
+        sent = blocks[place ^ hop]
+        outs.append(lax.ppermute(sent, "lev", [(i, i ^ hop) for i in range(peers)]))
+    blocks = jnp.stack(outs)[place ^ jnp.arange(peers)]
+    columns = laid_out(blocks, 1)
     level_count = columns.shape[1]
     column_count = columns.shape[2]
     profile_len = field_count * level_count

time: 256 us -> 239 us (0.934)
  local copies, waits for them, and re-layouts: 63.8 us -> 47.8 us
    unnamed x18 -> x19, local copies, waits for them, and re-layouts: 15.9 us -> 0.39 us
    all_to_all x1 -> x0, waiting for transfers between devices: 12 us -> none  [on_device(): lax.all_to_all(increment, 'lev', split_axis=2, concat_axis=1, tiled=True)]
    ppermute x0 -> x3, waiting for transfers between devices: none -> 11 us  [on_device(): outs.append(lax.ppermute(sent, 'lev', [(i, i ^ hop) for i in range(peers)]))]
    all_to_all x1 -> x0, local copies, waits for them, and re-layouts: 5.34 us -> none  [on_device(): lax.all_to_all(increment, 'lev', split_axis=2, concat_axis=1, tiled=True)]
    ppermute x0 -> x3, starting transfers between devices: none -> 4.94 us  [on_device(): outs.append(lax.ppermute(sent, 'lev', [(i, i ^ hop) for i in range(peers)]))]
    all_to_all x1 -> x0, starting transfers between devices: 4.55 us -> none  [on_device(): lax.all_to_all(increment, 'lev', split_axis=2, concat_axis=1, tiled=True)]
  transfers between devices with their start and end apart: 3 -> 5, of which waited for: 2 -> 4; matrix products, arithmetic and copies ran while one was open for 8% -> 9% of each run, Pallas kernels for 0% -> 0%
where the time goes in v1:
time: 239 us; the launch traced here: 238 us
  other arithmetic  57.7 us (24%)
  local copies, waits for them, and re-layouts  47.8 us (20%)
  matrix products  45.3 us (19%)
  waiting for transfers between devices  35.6 us (15%)
  blocking collectives  28.6 us (12%)
  starting transfers between devices  23.1 us (10%)
    scatter-add x1, other arithmetic, on_device(): jax.ops.segment_sum(adjoint, obs_slot, num_segments=peer_count * capacity)  50.4 us
    gather x1, local copies, waits for them, and re-layouts, on_device(): profile = incoming[obs_slot]  33.1 us
    all_to_all x1, blocking collectives, on_device(): lax.all_to_all(field_adjoint, 'lev', split_axis=1, concat_axis=2, tiled=T...  28.6 us
    all_to_all x1, waiting for transfers between devices, return_rows(): lax.all_to_all(outgoing, ('lev', 'col'), split_axis=0, concat_axis=0, til...  24.7 us
    dot_general x1, matrix products, observe(): jnp.einsum('tcf,cto->tof', jacobian, forcing, preferred_element_type=jnp....  24.5 us
    dot_general x1, matrix products, observe(): jnp.dot(bias_coef, predictor, precision=lax.Precision.HIGHEST, preferred_...  20.8 us
    ppermute x3, waiting for transfers between devices, on_device(): outs.append(lax.ppermute(sent, 'lev', [(i, i ^ hop) for i in range(peers)]))  11 us
    all_to_all x1, starting transfers between devices, return_rows(): lax.all_to_all(outgoing, ('lev', 'col'), split_axis=0, concat_axis=0, til...  9.6 us
  transfers between devices with their start and end apart: 5, of which 4 were waited for; matrix products, arithmetic and copies ran while one was open for 9% of the time, Pallas kernels for 0%

profile of v1, /device:TPU:0, one launch (start us, length us, event | category | flops | bytes accessed | tf_op | source)
XLA Modules:
  0.0 238.4 jit_solution(13486764975508423433)
XLA Ops:
  0.0 0.0 copy-start
  0.0 0.0 copy-start.5
  0.0 0.0 copy-start.2
  0.0 0.0 copy-start.4
  0.0 2.4 reshape.77
  2.4 1.8 constant_dynamic-slice_fusion.3
  4.2 0.1 copy.53
  4.3 1.7 collective-permute-start
  6.1 0.1 copy.52
  6.1 3.0 %collective-permute-start.1 = (bf16[3,32,1024]{2,1,0:T(8,128)(2,1)S(1)}, bf16[3,32,1024]{2,1,0:T(8,128)(2,1)S(1)}, u32[]{:S(2)}, u32[]{:S(2)}) collective-permute-start(bf16[3,32,1024]{2,1,0:T(8,128)(2,1)S(1)} %bitcast.71), channel_id=1, source_target_pairs={{0,64},{32,96},{64,0},{96,32},{1,65},{33,97},{65,1},{97,33},{2,66}... | collective-permute-start | bytes 589832 | tf_op jit(solution)/shard_map/ppermute | solution.py:74
  9.1 0.1 copy.51
  9.2 0.2 collective-permute-start.2
  9.4 0.1 copy.54
  9.5 0.0 copy-done.5
  9.5 0.1 copy.33
  9.6 0.1 reshape.95
  9.7 0.0 copy-done.2
  9.7 0.0 copy-done.6
  9.7 0.0 copy-done.4
  9.8 2.4 %collective-permute-done = bf16[3,32,1024]{2,1,0:T(8,128)(2,1)S(1)} collective-permute-done((bf16[3,32,1024]{2,1,0:T(8,128)(2,1)S(1)}, bf16[3,32,1024]{2,1,0:T(8,128)(2,1)S(1)}, u32[]{:S(2)}, u32[]{:S(2)}) %collective-permute-start) | collective-permute-done | bytes 196640 | tf_op jit(solution)/shard_map/ppermute | solution.py:74
  12.2 5.7 %collective-permute-done.1 = bf16[3,32,1024]{2,1,0:T(8,128)(2,1)S(1)} collective-permute-done((bf16[3,32,1024]{2,1,0:T(8,128)(2,1)S(1)}, bf16[3,32,1024]{2,1,0:T(8,128)(2,1)S(1)}, u32[]{:S(2)}, u32[]{:S(2)}) %collective-permute-start.1) | collective-permute-done | bytes 196640 | tf_op jit(solution)/shard_map/ppermute | solution.py:74
  17.9 2.9 %collective-permute-done.2 = bf16[3,32,1024]{2,1,0:T(8,128)(2,1)S(1)} collective-permute-done((bf16[3,32,1024]{2,1,0:T(8,128)(2,1)S(1)}, bf16[3,32,1024]{2,1,0:T(8,128)(2,1)S(1)}, u32[]{:S(2)}, u32[]{:S(2)}) %collective-permute-start.2) | collective-permute-done | bytes 196640 | tf_op jit(solution)/shard_map/ppermute | solution.py:74
  20.8 0.1 pad_maximum_fusion
  20.9 0.6 gather_fusion
  21.5 0.1 copy.31
  21.5 0.4 copy.32
  21.9 0.0 copy-start.3
  21.9 5.0 %gather_fusion.1 = bf16[1024,384]{1,0:T(8,128)(2,1)} fusion(bf16[1024,384]{1,0:T(8,128)(2,1)S(1)} %bitcast.58, s32[1024]{0:T(1024)S(1)} %broadcast_clamp_fusion), kind=kCustom, calls=%fused_computation.1 | custom fusion | bytes 1576960 | tf_op jit(solution)/shard_map/gather | solution.py:82
  26.9 8.6 %all-to-all-start = ((bf16[128,8,384]{2,1,0:T(8,128)(2,1)}), bf16[128,8,384]{2,1,0:T(8,128)(2,1)S(1)}, u32[]{:S(2)}, u32[]{:S(2)}) async-start(bf16[128,8,384]{2,1,0:T(8,128)(2,1)} %bitcast.9), calls=%async_computation | async-start | bytes 1572864 | tf_op jit(solution)/shard_map/all_to_all | solution.py:20
  35.5 0.0 copy-done
  35.5 0.0 copy-done.3
  35.5 20.8 %convert_subtract_fusion = f32[616,8192]{1,0:T(8,128)} fusion(bf16[616,8192]{1,0:T(8,128)(2,1)} %param.11, f32[616,8]{0,1:T(8,128)S(1)} %copy-done.3, f32[8,8192]{1,0:T(8,128)S(1)} %copy-done), kind=kOutput, calls=%fused_computation.8 | convolution fusion | flops 494534656 | bytes 30559488 | tf_op jit(solution)/shard_map/dot_general | solution.py:39
  56.3 0.0 all-to-all-done
  56.3 33.1 %gather_fusion.2 = bf16[8192,384]{1,0:T(8,128)(2,1)} fusion(bf16[1024,384]{1,0:T(8,128)(2,1)S(1)} %bitcast.57, s32[8192]{0:T(1024)S(1)} %fusion.12), kind=kCustom, calls=%fused_computation.2 | custom fusion | bytes 12615680 | tf_op jit(solution)/shard_map/gather | solution.py:84
  89.4 24.5 %fusion.2 = f32[8,1024,384]{2,1,0:T(8,128)} fusion(bf16[8,616,384]{2,1,0:T(8,128)(2,1)} %param.10, f32[77,8,8,1024]{3,2,1,0:T(8,128)} %bitcast.59, f32[616,8]{0,1:T(8,128)S(1)} %multiply_bitcast_fusion, bf16[8,1024,384]{2,1,0:T(8,128)(2,1)} %bitcast.60), kind=kOutput, calls=%fused_computation.9 | convolution fusion | flops 7766212608 | bytes 42863872 | tf_op jit(solution)/shard_map/tcf,cto->tof/dot_general | solution.py:48
  113.9 50.4 %scatter_custom_fusion = f32[1024,384]{1,0:T(8,128)} fusion(s32[8192]{0:T(1024)S(1)} %copy-done.2, f32[8192,384]{1,0:T(8,128)} %bitcast.73, f32[]{:T(128)} %constant.10.clone.1), kind=kCustom, calls=%fused_computation.16 | custom fusion | flops 3145728 | bytes 1573376 | tf_op jit(solution)/shard_map/scatter-add | solution.py:86
  164.4 9.6 %all-to-all-start.1 = ((f32[128,8,384]{2,1,0:T(8,128)}), f32[128,8,384]{2,1,0:T(8,128)S(1)}, u32[]{:S(2)}, u32[]{:S(2)}) async-start(f32[128,8,384]{2,1,0:T(8,128)} %bitcast.14), calls=%async_computation.1 | async-start | bytes 3145728 | tf_op jit(solution)/shard_map/all_to_all | solution.py:24
  174.0 0.1 copy.30
  174.1 0.1 reshape.119
  174.2 24.7 %all-to-all-done.1 = f32[128,8,384]{2,1,0:T(8,128)S(1)} async-done(((f32[128,8,384]{2,1,0:T(8,128)}), f32[128,8,384]{2,1,0:T(8,128)S(1)}, u32[]{:S(2)}, u32[]{:S(2)}) %all-to-all-start.1) | async-done | bytes 1572896 | tf_op jit(solution)/shard_map/all_to_all | solution.py:24
  198.8 7.1 %scatter_custom_fusion.1 = f32[1024,384]{1,0:T(8,128)S(1)} fusion(s32[1024]{0:T(1024)S(1)} %reshape.119, f32[128,8,384]{2,1,0:T(8,128)S(1)} %all-to-all-done.1, f32[]{:T(128)} %constant.10.clone.1), kind=kCustom, calls=%fused_computation.12 | custom fusion | flops 393216 | bytes 3145732 | tf_op jit(solution)/shard_map/scatter-add | solution.py:88
  205.9 0.5 copy.35
  206.4 1.1 copy.36
  207.5 0.0 copy-start.1
  207.5 28.6 %all_to_all.28 = f32[3,128,1024]{2,0,1:T(4,128)S(1)} all-to-all(f32[3,128,1024]{2,0,1:T(4,128)S(1)} %copy.36), channel_id=1, replica_groups=mesh['lev'=4,'col'=32] {'lev'}, dimensions={1} | all-to-all | bytes 3145728 | tf_op jit(solution)/shard_map/all_to_all | solution.py:94
  236.1 0.9 copy.37
  237.0 1.3 copy.44
  238.4 0.0 copy-done.1
  (8 shorter events, 0.0 us)
Async XLA Ops:
  0.0 35.5 %copy-start = (f32[8,8192]{1,0:T(8,128)S(1)}, f32[8,8192]{1,0:T(8,128)}, u32[]{:S(2)}) copy-start(f32[8,8192]{1,0:T(8,128)} %param.12) | copy-start | bytes 786436
  0.0 9.5 %copy-start.5 = (s32[1,128,8]{1,2,0:T(8,128)S(1)}, s32[1,128,8]{1,2,0:T(8,128)}, u32[]{:S(2)}) copy-start(s32[1,128,8]{1,2,0:T(8,128)} %param.16) | copy-start | bytes 12292
  0.0 9.7 %copy-start.2 = (s32[8192]{0:T(1024)S(1)}, s32[8192]{0:T(1024)}, u32[]{:S(2)}) copy-start(s32[8192]{0:T(1024)} %param.17) | copy-start | bytes 98308
  0.0 9.7 %copy-start.6 = (f32[616]{0:T(1024)S(1)}, f32[616]{0:T(1024)}, u32[]{:S(2)}) copy-start(f32[616]{0:T(1024)} %param.14) | copy-start | bytes 7396
  0.0 9.7 %copy-start.4 = (s32[8,616]{1,0:T(8,128)S(1)}, s32[8,616]{1,0:T(8,128)}, u32[]{:S(2)}) copy-start(s32[8,616]{1,0:T(8,128)} %param.15) | copy-start | bytes 59140
  4.3 7.9 %collective-permute-start = (bf16[3,32,1024]{2,1,0:T(8,128)(2,1)S(1)}, bf16[3,32,1024]{2,1,0:T(8,128)(2,1)S(1)}, u32[]{:S(2)}, u32[]{:S(2)}) collective-permute-start(bf16[3,32,1024]{2,1,0:T(8,128)(2,1)S(1)} %bitcast.70), channel_id=1, source_target_pairs={{0,32},{32,0},{64,96},{96,64},{1,33},{33,1},{65,97},{97,65},{2,34}... | collective-permute-start | bytes 589832 | tf_op jit(solution)/shard_map/ppermute | solution.py:74
  6.1 11.8 %collective-permute-start.1 = (bf16[3,32,1024]{2,1,0:T(8,128)(2,1)S(1)}, bf16[3,32,1024]{2,1,0:T(8,128)(2,1)S(1)}, u32[]{:S(2)}, u32[]{:S(2)}) collective-permute-start(bf16[3,32,1024]{2,1,0:T(8,128)(2,1)S(1)} %bitcast.71), channel_id=1, source_target_pairs={{0,64},{32,96},{64,0},{96,32},{1,65},{33,97},{65,1},{97,33},{2,66}... | collective-permute-start | bytes 589832 | tf_op jit(solution)/shard_map/ppermute | solution.py:74
  9.2 11.6 %collective-permute-start.2 = (bf16[3,32,1024]{2,1,0:T(8,128)(2,1)S(1)}, bf16[3,32,1024]{2,1,0:T(8,128)(2,1)S(1)}, u32[]{:S(2)}, u32[]{:S(2)}) collective-permute-start(bf16[3,32,1024]{2,1,0:T(8,128)(2,1)S(1)} %bitcast.72), channel_id=1, source_target_pairs={{0,96},{32,64},{64,32},{96,0},{1,97},{33,65},{65,33},{97,1},{2,98}... | collective-permute-start | bytes 589832 | tf_op jit(solution)/shard_map/ppermute | solution.py:74
  21.9 13.6 %copy-start.3 = (f32[616,8]{0,1:T(8,128)S(1)}, f32[616,8]{0,1:T(8,128)}, u32[]{:S(2)}) copy-start(f32[616,8]{0,1:T(8,128)} %param.13) | copy-start | bytes 59140
  26.9 29.4 %all-to-all-start = ((bf16[128,8,384]{2,1,0:T(8,128)(2,1)}), bf16[128,8,384]{2,1,0:T(8,128)(2,1)S(1)}, u32[]{:S(2)}, u32[]{:S(2)}) async-start(bf16[128,8,384]{2,1,0:T(8,128)(2,1)} %bitcast.9), calls=%async_computation | async-start | bytes 1572864 | tf_op jit(solution)/shard_map/all_to_all | solution.py:20
  164.4 34.5 %all-to-all-start.1 = ((f32[128,8,384]{2,1,0:T(8,128)}), f32[128,8,384]{2,1,0:T(8,128)S(1)}, u32[]{:S(2)}, u32[]{:S(2)}) async-start(f32[128,8,384]{2,1,0:T(8,128)} %bitcast.14), calls=%async_computation.1 | async-start | bytes 3145728 | tf_op jit(solution)/shard_map/all_to_all | solution.py:24
  207.5 30.9 %copy-start.1 = (f32[8,8192]{1,0:T(8,128)S(1)}, f32[8,8192]{1,0:T(8,128)}, u32[]{:S(2)}) copy-start(f32[8,8192]{1,0:T(8,128)} %param.12) | copy-start | bytes 786436
